TPU v7x, 32 devices: a whole 2x2x4 slice. The times are simulated.
32 devices in a mesh: prow: 4 (over y, x), pcol: 8 (over z, core).
Axes of the slice: x: 2, y: 2, z: 4, core: 2. Of those that a mesh axis runs over, the one named last changes fastest.
Arguments:
- covariance: float32 [4, 16, 256, 8, 8, 256], P('prow', None, None, 'pcol'), may hold values from 0 to 3, as said below
Outputs:
- factored: float32 [4, 16, 256, 8, 8, 256], P('prow', None, None, 'pcol')
Inputs may be any that keep to these rules, and one draw needn't show every extreme that they name: covariance is symmetric and positive definite.
All inputs are finite; a program needn't handle non-finite values.
Results may differ from a plain program's by a relative error of at most 0.0003.
Values sent between devices are 32-bit elements; how exact they have to be, the bound alone decides.
A program may use at most 192 MiB of HBM per device.

v0:
```python
import jax
import jax.numpy as jnp
from jax import lax
from jax.sharding import PartitionSpec as P

PANELS = 2


def from_root(block, axis, owner):
    block = jnp.where(lax.axis_index(axis) == owner, block, jnp.zeros_like(block))
    return lax.psum(block, axis)


def solve_rows(factor, column):
    count, tile, _ = column.shape
    stacked = jnp.transpose(column, (2, 0, 1)).reshape(tile, count * tile)
    solved = jax.scipy.linalg.solve_triangular(factor, stacked, lower=True)
    return solved.reshape(tile, count, tile).transpose(1, 2, 0)


def outer_update(row_terms, col_terms):
    return jnp.einsum("rae,cbe->racb", row_terms, col_terms, precision=lax.Precision.HIGHEST)


def per_device(covariance):
    prows = lax.axis_size("prow")
    pcols = lax.axis_size("pcol")
    prow_at = lax.axis_index("prow")
    pcol_at = lax.axis_index("pcol")
    rt_count = covariance.shape[1]
    tile = covariance.shape[2]
    ct_count = covariance.shape[4]
    ratio = pcols // prows
    tiles = covariance.reshape(rt_count, tile, ct_count, tile)
    row_index = jnp.arange(rt_count, dtype=jnp.int32) * prows + prow_at
    col_index = jnp.arange(ct_count, dtype=jnp.int32) * pcols + pcol_at
    for panel in range(PANELS):
        tile_row = panel // prows
        tile_col = panel // pcols
        column = tiles[:, :, tile_col, :]
        keep = row_index[:, None, None]
        diagonal = from_root(column[tile_row], "prow", panel % prows)
        factor = jnp.linalg.cholesky(diagonal)
        solved = solve_rows(factor, column)
        local_rows = jnp.where(keep > panel, solved, jnp.where(keep == panel, factor[None], 0.0))
        panel_rows = from_root(local_rows, "pcol", panel % pcols)
        grouped = panel_rows.reshape(ct_count, ratio, tile, tile)
        candidate = lax.dynamic_index_in_dim(grouped, pcol_at // prows, 1, keepdims=False)
        panel_cols = from_root(candidate, "prow", pcol_at % prows)
        rows_term = jnp.where(keep > panel, panel_rows, 0.0)
        cols_term = jnp.where(col_index[:, None, None] > panel, panel_cols, 0.0)
        tiles = tiles - outer_update(rows_term, cols_term)
        owner = pcol_at == panel % pcols
        tiles = tiles.at[:, :, tile_col, :].set(
            jnp.where(owner, panel_rows, tiles[:, :, tile_col, :])
        )
        upper_mask = (row_index == panel)[:, None, None, None] & (col_index > panel)[
            None, None, :, None
        ]
        tiles = jnp.where(upper_mask, 0.0, tiles)
    return tiles.reshape(1, rt_count, tile, 1, ct_count, tile)


def solution(mesh):
    return jax.shard_map(
        per_device,
        mesh=mesh,
        in_specs=(P("prow", None, None, "pcol", None, None),),
        out_specs=P("prow", None, None, "pcol", None, None),
        check_vma=False,
    )
```

profile of v0, /device:TPU:0, one launch (start us, length us, event | category | flops | bytes accessed | tf_op | source)
XLA Modules:
  0.0 839.5 jit_solution(12242120617229582276)
XLA Ops:
  6.5 34.9 %copy.17 = f32[1,16,256,1,8,256]{2,5,4,1,3,0:T(8,128)} copy(f32[1,16,256,1,8,256]{5,4,3,2,1,0:T(8,128)} %param.8) | data formatting | bytes 67108864 | tf_op args[0]
  41.5 1.7 fusion.29
  43.2 4.6 slice_bitcast_fusion.3
  47.8 5.4 copy.19
  53.2 35.8 %all-reduce.8.cloned.1.call-done = f32[256,256]{0,1:T(8,128)} async-done(((f32[256,256]{0,1:T(8,128)}), f32[256,256]{0,1:T(8,128)}) %all-reduce.8.cloned.1.call-update) | async-done | bytes 262160 | tf_op jit(solution)/shard_map/psum | solution.py:11
  91.1 11.7 %cholesky.130 = f32[128,128]{1,0:T(8,128)S(1)} custom-call(f32[128,128]{1,0:T(8,128)S(1)} %cholesky.194), custom_call_target="Cholesky" | custom-call | tf_op jit(solution)/shard_map/jit(cholesky)/cholesky | solution.py:43
  102.8 9.8 %custom-call.13 = f32[1,128,128]{1,2,0:T(8,128)S(1)} custom-call(f32[1,128,128]{2,1,0:T(8,128)S(1)} %get-tuple-element.78), custom_call_target="InvertDiagBlocksLowerTriangular" | custom-call | tf_op jit(solution)/shard_map/jit(cholesky)/cholesky | solution.py:43
  113.1 11.7 %cholesky.147 = f32[128,128]{1,0:T(8,128)S(1)} custom-call(f32[128,128]{1,0:T(8,128)S(1)} %convolution_subtract_fusion.5), custom_call_target="Cholesky" | custom-call | tf_op jit(solution)/shard_map/jit(cholesky)/cholesky | solution.py:43
  126.9 3.9 while.6
  130.8 19.9 %custom-call.14 = f32[2,128,128]{1,2,0:T(8,128)S(1)} custom-call(f32[2,128,128]{2,1,0:T(8,128)S(1)} %get-tuple-element.45), custom_call_target="InvertDiagBlocksLowerTriangular" | custom-call | tf_op jit(solution)/shard_map/jit(_solve_triangular)/triangular_solve | solution.py:17
  150.7 3.7 fusion.14
  154.4 3.4 convolution_subtract_fusion.3
  157.9 2.0 fusion.40
  159.8 2.4 pad_maximum_fusion
  162.3 5.6 copy.20
  167.9 5.3 copy.21
  173.3 4.8 fusion.9
  178.3 96.6 %all-reduce.10.cloned.1.call-done = f32[16,256,256]{1,2,0:T(8,128)} async-done(((f32[16,256,256]{1,2,0:T(8,128)}), f32[16,256,256]{1,2,0:T(8,128)}) %all-reduce.10.cloned.1.call-update) | async-done | bytes 4194320 | tf_op jit(solution)/shard_map/psum | solution.py:11
  274.9 3.1 constant_dynamic-slice_fusion.3
  277.9 2.3 copy.46
  282.0 69.7 %all-reduce.12.cloned.1.call-done = f32[8,256,256]{2,1,0:T(8,128)} async-done(((f32[8,256,256]{2,1,0:T(8,128)}), f32[8,256,256]{2,1,0:T(8,128)}) %all-reduce.12.cloned.1.call-update) | async-done | bytes 2097168 | tf_op jit(solution)/shard_map/psum | solution.py:11
  351.7 40.6 %convolution_subtract_fusion.1 = f32[16,256,8,256]{1,3,2,0:T(8,128)} fusion(f32[16,256,256]{1,2,0:T(8,128)} %all-reduce.10.cloned.1.call-done, f32[8,256,256]{2,1,0:T(8,128)} %all-reduce.12.cloned.1.call-done, pred[16]{0:T(512)(128)(4,1)S(1)} %get-tuple-element.83, pred[8]{0:T(512)(128)(4,1)S(1)} %fusion.45, f32[1,16,256,1,8,256]{2,5,4,1,3,0:T(8,128)} %copy.17), kind=kOutput, calls=%fused_computation.7 | convolution fusion | flops 25779765248 | bytes 73400344 | tf_op jit(solution)/shard_map/rae,cbe->racb/dot_general | solution.py:22
  392.3 4.7 fusion.5
  397.0 13.3 %broadcast_select_fusion = f32[16,256,8,256]{1,3,2,0:T(8,128)S(1)} fusion(f32[16,256,8,256]{1,3,2,0:T(8,128)} %fusion.5, pred[16,8]{1,0:T(8,128)(4,1)S(1)} %broadcast_and_fusion), kind=kLoop, calls=%fused_computation.5 | loop fusion | flops 8388608 | bytes 67108992 | tf_op jit(solution)/shard_map/jit(_where)/select_n | solution.py:60
  410.4 11.7 %copy-done = f32[16,256,8,256]{1,3,2,0:T(8,128)} copy-done((f32[16,256,8,256]{1,3,2,0:T(8,128)}, f32[16,256,8,256]{1,3,2,0:T(8,128)S(1)}, u32[]{:S(2)}) %copy-start) | copy-done | bytes 33554456
  422.8 4.6 slice_bitcast_fusion.1
  427.4 5.5 copy.29
  432.9 32.9 %all-reduce.14.cloned.1.call-done = f32[256,256]{0,1:T(8,128)} async-done(((f32[256,256]{0,1:T(8,128)}), f32[256,256]{0,1:T(8,128)}) %all-reduce.14.cloned.1.call-update) | async-done | bytes 262160 | tf_op jit(solution)/shard_map/psum | solution.py:11
  468.0 11.7 %cholesky.164 = f32[128,128]{1,0:T(8,128)S(1)} custom-call(f32[128,128]{1,0:T(8,128)S(1)} %cholesky.197), custom_call_target="Cholesky" | custom-call | tf_op jit(solution)/shard_map/jit(cholesky)/cholesky | solution.py:43
  479.7 9.8 %custom-call.15 = f32[1,128,128]{1,2,0:T(8,128)S(1)} custom-call(f32[1,128,128]{2,1,0:T(8,128)S(1)} %get-tuple-element.74), custom_call_target="InvertDiagBlocksLowerTriangular" | custom-call | tf_op jit(solution)/shard_map/jit(cholesky)/cholesky | solution.py:43
  490.0 11.7 %cholesky.181 = f32[128,128]{1,0:T(8,128)S(1)} custom-call(f32[128,128]{1,0:T(8,128)S(1)} %convolution_subtract_fusion.4), custom_call_target="Cholesky" | custom-call | tf_op jit(solution)/shard_map/jit(cholesky)/cholesky | solution.py:43
  504.4 3.9 while.7
  508.3 19.9 %custom-call.16 = f32[2,128,128]{1,2,0:T(8,128)S(1)} custom-call(f32[2,128,128]{2,1,0:T(8,128)S(1)} %get-tuple-element.46), custom_call_target="InvertDiagBlocksLowerTriangular" | custom-call | tf_op jit(solution)/shard_map/jit(_solve_triangular)/triangular_solve | solution.py:17
  528.2 3.7 fusion.12
  531.9 3.4 convolution_subtract_fusion.2
  535.3 2.0 fusion.36
  537.3 2.4 pad_maximum_fusion.1
  539.7 5.6 copy.30
  545.3 5.3 copy.31
  550.8 4.8 fusion.8
  555.7 96.6 %all-reduce.16.cloned.1.call-done = f32[16,256,256]{1,2,0:T(8,128)} async-done(((f32[16,256,256]{1,2,0:T(8,128)}), f32[16,256,256]{1,2,0:T(8,128)}) %all-reduce.16.cloned.1.call-update) | async-done | bytes 4194320 | tf_op jit(solution)/shard_map/psum | solution.py:11
  652.4 3.1 constant_dynamic-slice_fusion.2
  655.4 2.1 copy.48
  659.2 69.8 %all-reduce.18.cloned.1.call-done = f32[8,256,256]{2,1,0:T(8,128)} async-done(((f32[8,256,256]{2,1,0:T(8,128)}), f32[8,256,256]{2,1,0:T(8,128)}) %all-reduce.18.cloned.1.call-update) | async-done | bytes 2097168 | tf_op jit(solution)/shard_map/psum | solution.py:11
  729.0 40.6 %convolution_subtract_fusion = f32[16,256,8,256]{1,3,2,0:T(8,128)} fusion(f32[16,256,8,256]{1,3,2,0:T(8,128)} %copy-done, f32[16,256,256]{1,2,0:T(8,128)} %all-reduce.16.cloned.1.call-done, f32[8,256,256]{2,1,0:T(8,128)} %all-reduce.18.cloned.1.call-done, pred[16]{0:T(512)(128)(4,1)S(1)} %get-tuple-element.85, pred[8]{0:T(512)(128)(4,1)S(1)} %fusion.46), kind=kOutput, calls=%fused_computation.6 | convolution fusion | flops 25779765248 | bytes 73400344 | tf_op jit(solution)/shard_map/rae,cbe->racb/dot_general | solution.py:22
  769.6 4.7 fusion.2
  774.3 22.9 %select_bitcast_fusion = f32[1,16,256,1,8,256]{2,5,4,1,3,0:T(8,128)} fusion(f32[16,256,8,256]{1,3,2,0:T(8,128)} %fusion.2, pred[16,8]{1,0:T(8,128)(4,1)S(1)} %broadcast_and_fusion.1), kind=kLoop, calls=%fused_computation.4 | loop fusion | flops 8388608 | bytes 67108992 | tf_op jit(solution)/shard_map/reshape | solution.py:61
  797.2 34.9 %copy.37 = f32[1,16,256,1,8,256]{5,4,3,2,1,0:T(8,128)} copy(f32[1,16,256,1,8,256]{2,5,4,1,3,0:T(8,128)} %select_bitcast_fusion) | data formatting | bytes 67108864 | tf_op jit(solution)/shard_map/reshape | solution.py:61
  (69 shorter events, 19.7 us)
Async XLA Ops:
  6.5 82.4 %all-reduce.8.cloned.1.call-start = ((), (), s32[]{:S(2)}) async-start(), calls=%async_computation | async-start | bytes 524288 | tf_op jit(solution)/shard_map/psum | solution.py:11
  43.2 231.7 %all-reduce.10.cloned.1.call-start = ((), (), s32[]{:S(2)}) async-start(), calls=%async_computation.1 | async-start | bytes 8388608 | tf_op jit(solution)/shard_map/psum | solution.py:11
  150.7 3.7 copy-start.3
  178.2 173.5 %all-reduce.12.cloned.1.call-start = ((), (), s32[]{:S(2)}) async-start(), calls=%async_computation.2 | async-start | bytes 4194304 | tf_op jit(solution)/shard_map/psum | solution.py:11
  281.8 184.0 %all-reduce.14.cloned.1.call-start = ((), (), s32[]{:S(2)}) async-start(), calls=%async_computation.3 | async-start | bytes 524288 | tf_op jit(solution)/shard_map/psum | solution.py:11
  351.7 40.6 %copy-start.1 = (f32[16,256,256]{1,2,0:T(8,128)S(1)}, f32[16,256,256]{1,2,0:T(8,128)}, u32[]{:S(2)}) copy-start(f32[16,256,256]{1,2,0:T(8,128)} %all-reduce.10.cloned.1.call-done) | copy-start | bytes 12582916
  410.3 11.7 %copy-start = (f32[16,256,8,256]{1,3,2,0:T(8,128)}, f32[16,256,8,256]{1,3,2,0:T(8,128)S(1)}, u32[]{:S(2)}) copy-start(f32[16,256,8,256]{1,3,2,0:T(8,128)S(1)} %broadcast_select_fusion) | copy-start | bytes 100663296
  422.8 229.6 %all-reduce.16.cloned.1.call-start = ((), (), s32[]{:S(2)}) async-start(), calls=%async_computation.4 | async-start | bytes 8388608 | tf_op jit(solution)/shard_map/psum | solution.py:11
  528.2 3.7 copy-start.4
  555.7 173.3 %all-reduce.18.cloned.1.call-start = ((), (), s32[]{:S(2)}) async-start(), calls=%async_computation.5 | async-start | bytes 4194304 | tf_op jit(solution)/shard_map/psum | solution.py:11
  729.0 40.6 %copy-start.2 = (f32[16,256,256]{1,2,0:T(8,128)S(1)}, f32[16,256,256]{1,2,0:T(8,128)}, u32[]{:S(2)}) copy-start(f32[16,256,256]{1,2,0:T(8,128)} %all-reduce.16.cloned.1.call-done) | copy-start | bytes 12582916
Sparse Core Ops, SparseCore 0:
  43.3 45.6 all-reduce.7
  178.3 96.5 all-reduce.9
  282.0 69.6 all-reduce.11
  422.9 42.9 all-reduce.13
  555.8 96.5 all-reduce.15
  659.3 69.6 all-reduce.17
where the time goes:
time: 850 us; the launch traced here: 839 us
  waiting for transfers between devices  402 us (47%)
  other arithmetic  176 us (21%)
  local copies, waits for them, and re-layouts  144 us (17%)
  matrix products  100 us (12%)
  between operations  16.7 us (2%)
    psum x6, waiting for transfers between devices, from_root(): return lax.psum(block, axis)  401 us
    dot_general x2, matrix products, outer_update(): jnp.einsum('rae,cbe->racb', row_terms, col_terms, precision=lax.Precision...  81.1 us
    another operation x13, other arithmetic, per_device(): factor = jnp.linalg.cholesky(diagonal)  68.6 us
    unnamed x13, local copies, waits for them, and re-layouts  51.1 us
    another operation x7, other arithmetic, solve_rows(): solved = jax.scipy.linalg.solve_triangular(factor, stacked, lower=True)  44.7 us
    reshape x1, local copies, waits for them, and re-layouts, per_device(): return tiles.reshape(1, rt_count, tile, 1, ct_count, tile)  34.9 us
    reshape x1, other arithmetic, per_device(): return tiles.reshape(1, rt_count, tile, 1, ct_count, tile)  22.9 us
    transpose x4, local copies, waits for them, and re-layouts, solve_rows(): stacked = jnp.transpose(column, (2, 0, 1)).reshape(tile, count * tile)  20 us
  transfers between devices with their start and end apart: 6, of which 6 were waited for; matrix products, arithmetic and copies ran while one was open for 2% of the time, Pallas kernels for 0%

commit v1 on v0

v1 whole, which is shorter than its diff:
```python
import jax
import jax.numpy as jnp
from jax import lax
from jax.experimental import pallas as pl
from jax.experimental.pallas import tpu as pltpu
from jax.sharding import PartitionSpec as P

PANELS = 2
CHUNKS = 8
HIGHEST = lax.Precision.HIGHEST


def rows_along_pcol(own, pcols, pcol_at):
    pairs = pcols // 2
    pair_at = pcol_at // 2
    perm = [(q, q + 2) for q in range(pcols - 2)]
    size = own.shape[0] // CHUNKS
    chunks = own.reshape((CHUNKS, size) + own.shape[1:])
    got = []
    for slot in range(CHUNKS + pairs - 2):
        first = chunks[min(slot, CHUNKS - 1)]
        send = first if slot == 0 else jnp.where(pair_at == 0, first, got[-1])
        got.append(lax.ppermute(send, "pcol", perm))
    stacked = jnp.stack(got)
    here = lax.dynamic_slice_in_dim(stacked, jnp.maximum(pair_at - 1, 0), CHUNKS, 0)
    mine = jnp.where(pair_at == 0, chunks, here).reshape(own.shape)
    other = lax.ppermute(mine, "pcol", [(q, q ^ 1) for q in range(pcols)])
    even = pcol_at % 2 == 0
    return jnp.where(even, mine, other), jnp.where(even, other, mine)


def cols_along_prow(own, prows, prow_at):
    mine = own
    width = 2
    while width < prows:
        got = lax.ppermute(mine, "prow", [(p, p + width) for p in range(width)])
        mine = jnp.where((prow_at >= width) & (prow_at < 2 * width), got, mine)
        width *= 2
    other = lax.ppermute(mine, "prow", [(p, p ^ 1) for p in range(prows)])
    even = prow_at % 2 == 0
    return jnp.concatenate([jnp.where(even, mine, other), jnp.where(even, other, mine)], 0)


def split(value):
    high = value.astype(jnp.bfloat16)
    low = (value - high.astype(jnp.float32)).astype(jnp.bfloat16)
    return high, low


def update_kernel(place, tiles_ref, rows_ref, cols_ref, out_ref, rows_all, cols_all):
    step = pl.program_id(0)
    depth = cols_ref.shape[0]
    count = tiles_ref.shape[2]
    tile = tiles_ref.shape[3]

    @pl.when(step == 0)
    def _():
        for c in range(count):
            at = pl.ds(c * tile, tile)
            high, low = split(cols_ref[:, at])
            cols_all[pl.ds(0, depth), at] = high
            cols_all[pl.ds(depth, depth), at] = low
            cols_all[pl.ds(2 * depth, depth), at] = high

    high, low = split(rows_ref[0])
    rows_all[:, pl.ds(0, depth)] = high
    rows_all[:, pl.ds(depth, depth)] = high
    rows_all[:, pl.ds(2 * depth, depth)] = low
    top = step * place[2] + place[0] < PANELS
    panel = place[1]
    for c in range(count):
        term = jnp.dot(
            rows_all[...], cols_all[:, pl.ds(c * tile, tile)], preferred_element_type=jnp.float32
        )
        value = jnp.where(top, 0.0, tiles_ref[0, :, c, :] - term)
        if c == 0:
            value = jnp.where(panel == 0, rows_ref[0, :, pl.ds(0, tile)], value)
            value = jnp.where(panel == 1, rows_ref[0, :, pl.ds(tile, tile)], value)
        out_ref[0, :, c, :] = value


def update(place, tiles, rows_term, cols_term):
    rt_count, tile, ct_count, _ = tiles.shape
    depth = cols_term.shape[0]
    block = pl.BlockSpec((1, tile, ct_count, tile), lambda r, place: (r, 0, 0, 0))
    size = 2 * tiles.size * 4
    return pl.pallas_call(
        update_kernel,
        grid_spec=pltpu.PrefetchScalarGridSpec(
            num_scalar_prefetch=1,
            grid=(rt_count,),
            in_specs=[
                block,
                pl.BlockSpec((1, tile, depth), lambda r, place: (r, 0, 0)),
                pl.BlockSpec((depth, ct_count * tile), lambda r, place: (0, 0)),
            ],
            out_specs=block,
            scratch_shapes=[
                pltpu.VMEM((tile, 3 * depth), jnp.bfloat16),
                pltpu.VMEM((3 * depth, ct_count * tile), jnp.bfloat16),
            ],
        ),
        out_shape=jax.ShapeDtypeStruct(tiles.shape, jnp.float32),
        compiler_params=pltpu.CompilerParams(vmem_limit_bytes=48 * 1024 * 1024),
        cost_estimate=pl.CostEstimate(
            flops=6 * depth * tiles.size, bytes_accessed=size, transcendentals=0
        ),
    )(place, tiles, rows_term, cols_term)


def per_device(covariance):
    prows = lax.axis_size("prow")
    pcols = lax.axis_size("pcol")
    prow_at = lax.axis_index("prow")
    pcol_at = lax.axis_index("pcol")
    rt_count = covariance.shape[1]
    tile = covariance.shape[2]
    ct_count = covariance.shape[4]
    tiles = covariance.reshape(rt_count, tile, ct_count, tile)

    corner = tiles[0, :, 0, :]
    inside = (prow_at < PANELS) & (pcol_at < PANELS)
    spots = [
        jnp.where(inside & (prow_at == i) & (pcol_at == j), corner, 0.0)
        for i, j in ((0, 0), (1, 0), (1, 1))
    ]
    a00, a10, a11 = lax.psum(jnp.stack(spots), ("prow", "pcol"))

    raw_cols = cols_along_prow(tiles[0].reshape(tile, ct_count * tile), prows, prow_at)
    raw_0, raw_1 = rows_along_pcol(tiles[:, :, 0, :].reshape(rt_count * tile, tile), pcols, pcol_at)

    eye = jnp.eye(tile, dtype=jnp.float32)
    l00 = jnp.linalg.cholesky(a00, symmetrize_input=False)
    i00 = jax.scipy.linalg.solve_triangular(l00, eye, lower=True)
    l10 = jnp.dot(a10, i00.T, precision=HIGHEST)
    l11 = jnp.linalg.cholesky(a11 - jnp.dot(l10, l10.T, precision=HIGHEST), symmetrize_input=False)
    i11 = jax.scipy.linalg.solve_triangular(l11, eye, lower=True)

    def solve(first, second):
        one = jnp.dot(first, i00.T, precision=HIGHEST)
        two = jnp.dot(second - jnp.dot(one, l10.T, precision=HIGHEST), i11.T, precision=HIGHEST)
        return one, two

    rows_0, rows_1 = solve(raw_0, raw_1)
    top = jnp.dot(i00, raw_cols[:tile], precision=HIGHEST)
    low = jnp.dot(
        i11, raw_cols[tile:] - jnp.dot(l10, top, precision=HIGHEST), precision=HIGHEST
    )
    cols_term = jnp.concatenate([top, low], 0)
    rows_term = jnp.concatenate([rows_0, rows_1], 1).reshape(rt_count, tile, 2 * tile)
    row_index = (jnp.arange(rt_count, dtype=jnp.int32) * prows + prow_at)[:, None, None]
    d0 = jnp.concatenate([l00, jnp.zeros_like(l00)], 1)
    d1 = jnp.concatenate([l10, l11], 1)
    rows_term = jnp.where(row_index == 0, d0, jnp.where(row_index == 1, d1, rows_term))

    place = jnp.stack([prow_at, pcol_at, jnp.int32(prows)]).astype(jnp.int32)
    out = update(place, tiles, rows_term, cols_term)
    return out.reshape(1, rt_count, tile, 1, ct_count, tile)


def solution(mesh):
    return jax.shard_map(
        per_device,
        mesh=mesh,
        in_specs=(P("prow", None, None, "pcol", None, None),),
        out_specs=P("prow", None, None, "pcol", None, None),
        check_vma=False,
    )
```

time: 850 us -> 496 us (0.58)
  waiting for transfers between devices: 402 us -> 117 us
  local copies, waits for them, and re-layouts: 144 us -> 73.5 us
  matrix products: 100 us -> 34.5 us
  Pallas kernels: 0 us -> 50.7 us
  starting transfers between devices: 0.21 us -> 49.5 us
  other arithmetic: 176 us -> 148 us
    psum x6 -> x1, waiting for transfers between devices: 401 us -> 82.5 us  [per_device(): a00, a10, a11 = lax.psum(jnp.stack(spots), ('prow', 'pcol'))]
    dot_general x2 -> x8, matrix products: 81.1 us -> 29.9 us  [the longest x1 7.18 us: solve(): jnp.dot(one, l10.T, precision=HIGHEST)]
    pallas_call x0 -> x1, Pallas kernels: none -> 50.7 us  [update(): pl.pallas_call(update_kernel, grid_spec=pltpu.PrefetchScalarGridSpec(num_...]
    ppermute x0 -> x13, starting transfers between devices: none -> 49.5 us  [the longest x10 41.8 us: rows_along_pcol(): got.append(lax.ppermute(send, 'pcol', perm))]
    reshape x3 -> x0, local copies, waits for them, and re-layouts: 45.6 us -> none  [the longest x1 34.9 us: per_device(): return tiles.reshape(1, rt_count, tile, 1, ct_count, tile)]
    ppermute x0 -> x13, waiting for transfers between devices: none -> 34 us  [the longest x10 33.5 us: rows_along_pcol(): got.append(lax.ppermute(send, 'pcol', perm))]
    unnamed x13 -> x56, local copies, waits for them, and re-layouts: 51.1 us -> 19 us
    slice x0 -> x3, local copies, waits for them, and re-layouts: none -> 28.9 us  [the longest x1 13.7 us: per_device(): tiles[:, :, 0, :].reshape(rt_count * tile, tile)]
  transfers between devices with their start and end apart: 6 -> 14, of which waited for: 6 -> 8; matrix products, arithmetic and copies ran while one was open for 2% -> 43% of each run, Pallas kernels for 0% -> 0%
where the time goes in v1:
time: 496 us; the launch traced here: 490 us
  other arithmetic  148 us (30%)
  waiting for transfers between devices  117 us (24%)
  local copies, waits for them, and re-layouts  73.5 us (15%)
  Pallas kernels  50.7 us (10%)
  starting transfers between devices  49.5 us (10%)
  matrix products  34.5 us (7%)
  between operations  16.8 us (3%)
    psum x1, waiting for transfers between devices, per_device(): a00, a10, a11 = lax.psum(jnp.stack(spots), ('prow', 'pcol'))  82.5 us
    pallas_call x1, Pallas kernels, update(): pl.pallas_call(update_kernel, grid_spec=pltpu.PrefetchScalarGridSpec(num_...  50.7 us
    ppermute x10, starting transfers between devices, rows_along_pcol(): got.append(lax.ppermute(send, 'pcol', perm))  41.8 us
    another operation x7, other arithmetic, per_device(): jnp.linalg.cholesky(a11 - jnp.dot(l10, l10.T, precision=HIGHEST), symmetr...  35.9 us
    another operation x6, other arithmetic, per_device(): l00 = jnp.linalg.cholesky(a00, symmetrize_input=False)  34 us
    ppermute x10, waiting for transfers between devices, rows_along_pcol(): got.append(lax.ppermute(send, 'pcol', perm))  33.5 us
    another operation x2, other arithmetic, per_device(): i11 = jax.scipy.linalg.solve_triangular(l11, eye, lower=True)  21.4 us
    another operation x3, other arithmetic, per_device(): i00 = jax.scipy.linalg.solve_triangular(l00, eye, lower=True)  20.4 us
  transfers between devices with their start and end apart: 14, of which 8 were waited for; matrix products, arithmetic and copies ran while one was open for 43% of the time, Pallas kernels for 0%

profile of v1, /device:TPU:0, one launch (start us, length us, event | category | flops | bytes accessed | tf_op | source)
XLA Modules:
  0.0 489.9 jit_solution(8596918759667948877)
XLA Ops:
  8.3 1.9 fusion.14
  14.5 6.2 %collective-permute-start.11 = (f32[256,2048]{1,0:T(8,128)S(1)}, f32[256,2048]{1,0:T(8,128)}, u32[]{:S(2)}, u32[]{:S(2)}) collective-permute-start(f32[256,2048]{1,0:T(8,128)S(1)} %bitcast.131), channel_id=1, source_target_pairs={{0,16},{8,24},{1,17},{9,25},{2,18},{10,26},{3,19},{11,27},{4,20},{... | collective-permute-start | bytes 6291464 | tf_op jit(solution)/shard_map/ppermute | solution.py:36
  20.8 13.5 %fusion.46 = (f32[2,256,1,256]{3,2,1,0:T(1,128)}, f32[2,256,1,256]{3,2,1,0:T(1,128)}, f32[2,256,1,256]{3,2,1,0:T(1,128)}, f32[2,256,1,256]{3,2,1,0:T(1,128)}, f3...) fusion(f32[16,256,8,256]{3,2,1,0:T(8,128)} %bitcast.136), kind=kLoop, calls=%fused_computation.114 | loop fusion | bytes 8388608 | tf_op jit(solution)/shard_map/slice | solution.py:21
  35.1 4.4 collective-permute-start
  39.7 13.7 %slice.110 = f32[16,256,1,256]{3,2,1,0:T(1,128)} slice(f32[16,256,8,256]{3,2,1,0:T(8,128)} %bitcast.137), slice={[0:16], [0:256], [0:1], [0:256]} | slice | bytes 8388608 | tf_op jit(solution)/shard_map/slice | solution.py:130
  53.4 4.7 copy.13
  63.2 82.5 %all-reduce.4.cloned.1.call-done = f32[3,256,256]{2,0,1:T(4,128)} async-done(((f32[3,256,256]{2,0,1:T(4,128)}), f32[3,256,256]{2,0,1:T(4,128)}) %all-reduce.4.cloned.1.call-update) | async-done | bytes 786448 | tf_op jit(solution)/shard_map/psum | solution.py:127
  145.7 3.8 fusion.47
  149.5 11.7 %cholesky.133 = f32[128,128]{1,0:T(8,128)S(1)} custom-call(f32[128,128]{1,0:T(8,128)S(1)} %cholesky.199), custom_call_target="Cholesky" | custom-call | tf_op jit(solution)/shard_map/jit(cholesky)/cholesky | solution.py:133
  161.3 9.8 %custom-call.13 = f32[1,128,128]{1,2,0:T(8,128)S(1)} custom-call(f32[1,128,128]{2,1,0:T(8,128)S(1)} %get-tuple-element.67), custom_call_target="InvertDiagBlocksLowerTriangular" | custom-call | tf_op jit(solution)/shard_map/jit(cholesky)/cholesky | solution.py:133
  171.1 2.0 bitcast_select_fusion.8
  173.1 4.5 collective-permute-start.1
  178.3 11.7 %cholesky.150 = f32[128,128]{1,0:T(8,128)S(1)} custom-call(f32[128,128]{1,0:T(8,128)S(1)} %convolution_subtract_fusion.4), custom_call_target="Cholesky" | custom-call | tf_op jit(solution)/shard_map/jit(cholesky)/cholesky | solution.py:133
  190.1 1.9 bitcast_select_fusion.7
  192.0 2.6 collective-permute-start.2
  197.3 6.2 %collective-permute-done.2 = f32[512,256]{1,0:T(8,128)} collective-permute-done((f32[512,256]{1,0:T(8,128)}, f32[512,256]{1,0:T(8,128)}, u32[]{:S(2)}, u32[]{:S(2)}) %collective-permute-start.2) | collective-permute-done | bytes 524320 | tf_op jit(solution)/shard_map/ppermute | solution.py:23
  205.4 5.3 %collective-permute-start.3 = (f32[512,256]{1,0:T(8,128)}, f32[512,256]{1,0:T(8,128)}, u32[]{:S(2)}, u32[]{:S(2)}) collective-permute-start(f32[512,256]{1,0:T(8,128)} %bitcast_select_fusion.6), channel_id=1, source_target_pairs={{0,2},{1,3},{2,4},{3,5},{4,6},{5,7},{8,10},{9,11},{10,12},{11,13},... | collective-permute-start | bytes 1572872 | tf_op jit(solution)/shard_map/ppermute | solution.py:23
  210.9 4.1 while.4
  215.0 19.7 %custom-call.14 = f32[2,128,128]{1,2,0:T(8,128)S(1)} custom-call(f32[2,128,128]{2,1,0:T(8,128)S(1)} %get-tuple-element.21), custom_call_target="InvertDiagBlocksLowerTriangular" | custom-call | tf_op jit(solution)/shard_map/jit(_solve_triangular)/triangular_solve | solution.py:134
  235.8 2.4 collective-permute-start.4
  239.1 7.0 %collective-permute-done.4 = f32[512,256]{1,0:T(8,128)S(1)} collective-permute-done((f32[512,256]{1,0:T(8,128)S(1)}, f32[512,256]{1,0:T(8,128)S(1)}, u32[]{:S(2)}, u32[]{:S(2)}) %collective-permute-start.4) | collective-permute-done | bytes 524320 | tf_op jit(solution)/shard_map/ppermute | solution.py:23
  246.2 2.1 bitcast_select_fusion.4
  248.3 5.6 %collective-permute-start.5 = (f32[512,256]{1,0:T(8,128)}, f32[512,256]{1,0:T(8,128)}, u32[]{:S(2)}, u32[]{:S(2)}) collective-permute-start(f32[512,256]{1,0:T(8,128)} %bitcast_select_fusion.4), channel_id=1, source_target_pairs={{0,2},{1,3},{2,4},{3,5},{4,6},{5,7},{8,10},{9,11},{10,12},{11,13},... | collective-permute-start | bytes 1572872 | tf_op jit(solution)/shard_map/ppermute | solution.py:23
  257.6 11.7 %cholesky.168 = f32[128,128]{1,0:T(8,128)S(1)} custom-call(f32[128,128]{1,0:T(8,128)S(1)} %cholesky.202), custom_call_target="Cholesky" | custom-call | tf_op jit(solution)/shard_map/jit(cholesky)/cholesky | solution.py:136
  269.3 10.4 %custom-call.15 = f32[1,128,128]{1,2,0:T(8,128)} custom-call(f32[1,128,128]{2,1,0:T(8,128)S(1)} %get-tuple-element.63), custom_call_target="InvertDiagBlocksLowerTriangular" | custom-call | tf_op jit(solution)/shard_map/jit(cholesky)/cholesky | solution.py:136
  281.7 2.6 collective-permute-start.6
  288.3 2.6 collective-permute-done.6
  291.0 5.4 %collective-permute-start.7 = (f32[512,256]{1,0:T(8,128)S(1)}, f32[512,256]{1,0:T(8,128)S(1)}, u32[]{:S(2)}, u32[]{:S(2)}) collective-permute-start(f32[512,256]{1,0:T(8,128)S(1)} %bitcast_select_fusion.2), channel_id=1, source_target_pairs={{0,2},{1,3},{2,4},{3,5},{4,6},{5,7},{8,10},{9,11},{10,12},{11,13},... | collective-permute-start | bytes 1572872 | tf_op jit(solution)/shard_map/ppermute | solution.py:23
  299.6 5.1 %collective-permute-done.7 = f32[512,256]{1,0:T(8,128)S(1)} collective-permute-done((f32[512,256]{1,0:T(8,128)S(1)}, f32[512,256]{1,0:T(8,128)S(1)}, u32[]{:S(2)}, u32[]{:S(2)}) %collective-permute-start.7) | collective-permute-done | bytes 524320 | tf_op jit(solution)/shard_map/ppermute | solution.py:23
  304.8 4.4 collective-permute-start.8
  311.6 7.0 %collective-permute-done.8 = f32[512,256]{1,0:T(8,128)S(1)} collective-permute-done((f32[512,256]{1,0:T(8,128)S(1)}, f32[512,256]{1,0:T(8,128)S(1)}, u32[]{:S(2)}, u32[]{:S(2)}) %collective-permute-start.8) | collective-permute-done | bytes 524320 | tf_op jit(solution)/shard_map/ppermute | solution.py:23
  318.8 4.4 collective-permute-start.9
  324.4 5.5 %collective-permute-done.9 = f32[512,256]{1,0:T(8,128)S(1)} collective-permute-done((f32[512,256]{1,0:T(8,128)S(1)}, f32[512,256]{1,0:T(8,128)S(1)}, u32[]{:S(2)}, u32[]{:S(2)}) %collective-permute-start.9) | collective-permute-done | bytes 524320 | tf_op jit(solution)/shard_map/ppermute | solution.py:23
  329.9 2.7 dynamic-slice_select_fusion
  336.0 11.7 %cholesky.185 = f32[128,128]{1,0:T(8,128)S(1)} custom-call(f32[128,128]{1,0:T(8,128)S(1)} %convolution_subtract_fusion.3), custom_call_target="Cholesky" | custom-call | tf_op jit(solution)/shard_map/jit(cholesky)/cholesky | solution.py:136
  352.0 4.2 while.5
  356.2 19.7 %custom-call.16 = f32[2,128,128]{1,2,0:T(8,128)S(1)} custom-call(f32[2,128,128]{2,1,0:T(8,128)S(1)} %get-tuple-element.22), custom_call_target="InvertDiagBlocksLowerTriangular" | custom-call | tf_op jit(solution)/shard_map/jit(_solve_triangular)/triangular_solve | solution.py:137
  381.1 2.0 fusion.8
  383.1 1.9 fusion.49
  385.1 3.7 fusion.5
  388.8 2.4 pad_maximum_fusion.1.cols_ref
  391.2 6.1 %fusion.3 = f32[4096,256]{0,1:T(8,128)S(1)} fusion(f32[4096,256]{1,0:T(8,128)} %bitcast.27, f32[4096,256]{1,0:T(8,128)} %collective-permute-done.10, pred[]{:T(512)S(6)} %eq.63, f32[128,256]{1,0:T(8,128)S(1)} %fusion.32, f32[128,256]{1,0:T(8,128)S(1)} %fusion.25), kind=kOutput, calls=%fused_computation.10 | convolution fusion | flops 3222339584 | bytes 12845057 | tf_op jit(solution)/shard_map/dot_general | solution.py:140
  397.4 7.2 %fusion.48 = f32[4096,256]{1,0:T(8,128)S(1)} fusion(f32[4096,256]{0,1:T(8,128)S(1)} %fusion.3, f32[256,256]{0,1:T(8,128)S(1)} %fusion.17), kind=kOutput, calls=%fused_computation.116 | convolution fusion | flops 3221225472 | bytes 8650752 | tf_op jit(solution)/shard_map/dot_general | solution.py:141
  404.5 6.0 %fusion = f32[4096,256]{0,1:T(8,128)S(1)} fusion(f32[4096,256]{1,0:T(8,128)S(1)} %fusion.48, f32[4096,256]{1,0:T(8,128)} %collective-permute-done.10, f32[4096,256]{1,0:T(8,128)} %bitcast.27, pred[]{:T(512)S(6)} %eq.63, f32[128,256]{1,0:T(8,128)S(1)} %fusion.28, f32[128,256]{1,0:T(8,128)S(1)} %fusion.23), kind=kOutput, calls=%fused_computation.7 | convolution fusion | flops 3223388160 | bytes 17039360 | tf_op jit(solution)/shard_map/dot_general | solution.py:141
  410.5 3.9 pad_maximum_fusion
  414.5 9.1 %copy.8 = f32[4096,512]{1,0:T(8,128)} copy(f32[4096,512]{0,1:T(8,128)} %pad_maximum_fusion) | data formatting | bytes 16777216 | tf_op jit(solution)/shard_map/concatenate | solution.py:150
  423.6 8.5 %select_select_fusion.rows_ref = f32[16,256,512]{2,1,0:T(8,128)} fusion(f32[16,256,512]{2,1,0:T(8,128)} %bitcast.129, f32[256,512]{1,0:T(8,128)S(1)} %copy-done.11, f32[256,512]{1,0:T(8,128)S(1)} %copy-done.10, pred[16]{0:T(512)(128)(4,1)S(1)} %get-tuple-element.68, pred[16]{0:T(512)(128)(4,1)S(1)} %get-tuple-element.69), kind=kLoop, calls=%fused_computation.5 | loop fusion | flops 4194304 | bytes 17825824 | tf_op jit(solution)/shard_map/jit(_where)/select_n | solution.py:154
  432.1 50.7 %shard_map.17 = f32[16,256,8,256]{3,2,1,0:T(8,128)} custom-call(s32[3]{0:T(128)S(1)} %pad_add_fusion.place, f32[16,256,8,256]{3,2,1,0:T(8,128)} %bitcast.138, f32[16,256,512]{2,1,0:T(8,128)} %select_select_fusion.rows_ref, f32[512,2048]{1,0:T(8,128)S(1)} %copy-done), custom_call_target="tpu_custom_call" | custom-call | flops 25769803776 | bytes 67108864 | tf_op jit(solution)/shard_map/pallas_call | solution.py:87
  (128 shorter events, 54.5 us)
Async XLA Ops:
  6.5 139.2 %all-reduce.4.cloned.1.call-start = ((), (), s32[]{:S(2)}) async-start(), calls=%async_computation | async-start | bytes 2097152 | tf_op jit(solution)/shard_map/psum | solution.py:127
  14.5 19.7 %copy-start.2 = (f32[32,8,8,256]{3,1,2,0:T(8,128)}, f32[32,8,8,256]{3,1,2,0:T(8,128)S(1)}, u32[]{:S(2)}) copy-start(f32[32,8,8,256]{3,1,2,0:T(8,128)S(1)} %copy.22) | copy-start | bytes 6291460
  14.5 318.1 %collective-permute-start.11 = (f32[256,2048]{1,0:T(8,128)S(1)}, f32[256,2048]{1,0:T(8,128)}, u32[]{:S(2)}, u32[]{:S(2)}) collective-permute-start(f32[256,2048]{1,0:T(8,128)S(1)} %bitcast.131), channel_id=1, source_target_pairs={{0,16},{8,24},{1,17},{9,25},{2,18},{10,26},{3,19},{11,27},{4,20},{... | collective-permute-start | bytes 6291464 | tf_op jit(solution)/shard_map/ppermute | solution.py:36
  35.1 136.0 %collective-permute-start = (f32[512,256]{1,0:T(8,128)}, f32[512,256]{1,0:T(8,128)}, u32[]{:S(2)}, u32[]{:S(2)}) collective-permute-start(f32[512,256]{1,0:T(8,128)} %bitcast.44), channel_id=1, source_target_pairs={{0,2},{1,3},{2,4},{3,5},{4,6},{5,7},{8,10},{9,11},{10,12},{11,13},... | collective-permute-start | bytes 1572872 | tf_op jit(solution)/shard_map/ppermute | solution.py:23
  53.4 4.7 copy-start.9
  53.4 4.7 copy-start.8
  53.4 5.6 %copy-start.7 = (f32[2,256,1,256]{3,2,1,0:T(1,128)S(1)}, f32[2,256,1,256]{3,2,1,0:T(1,128)}, u32[]{:S(2)}) copy-start(f32[2,256,1,256]{3,2,1,0:T(1,128)} %get-tuple-element.51) | copy-start | bytes 1572868
  53.4 6.4 %copy-start.6 = (f32[2,256,1,256]{3,2,1,0:T(1,128)S(1)}, f32[2,256,1,256]{3,2,1,0:T(1,128)}, u32[]{:S(2)}) copy-start(f32[2,256,1,256]{3,2,1,0:T(1,128)} %get-tuple-element.52) | copy-start | bytes 1572868
  58.1 2.6 copy-start.5
  58.1 3.4 copy-start.4
  173.1 17.0 %collective-permute-start.1 = (f32[512,256]{1,0:T(8,128)}, f32[512,256]{1,0:T(8,128)}, u32[]{:S(2)}, u32[]{:S(2)}) collective-permute-start(f32[512,256]{1,0:T(8,128)} %bitcast_select_fusion.8), channel_id=1, source_target_pairs={{0,2},{1,3},{2,4},{3,5},{4,6},{5,7},{8,10},{9,11},{10,12},{11,13},... | collective-permute-start | bytes 1572872 | tf_op jit(solution)/shard_map/ppermute | solution.py:23
  192.0 11.6 %collective-permute-start.2 = (f32[512,256]{1,0:T(8,128)}, f32[512,256]{1,0:T(8,128)}, u32[]{:S(2)}, u32[]{:S(2)}) collective-permute-start(f32[512,256]{1,0:T(8,128)} %bitcast_select_fusion.7), channel_id=1, source_target_pairs={{0,2},{1,3},{2,4},{3,5},{4,6},{5,7},{8,10},{9,11},{10,12},{11,13},... | collective-permute-start | bytes 1572872 | tf_op jit(solution)/shard_map/ppermute | solution.py:23
  205.4 29.3 %collective-permute-start.3 = (f32[512,256]{1,0:T(8,128)}, f32[512,256]{1,0:T(8,128)}, u32[]{:S(2)}, u32[]{:S(2)}) collective-permute-start(f32[512,256]{1,0:T(8,128)} %bitcast_select_fusion.6), channel_id=1, source_target_pairs={{0,2},{1,3},{2,4},{3,5},{4,6},{5,7},{8,10},{9,11},{10,12},{11,13},... | collective-permute-start | bytes 1572872 | tf_op jit(solution)/shard_map/ppermute | solution.py:23
  215.0 23.6 %copy-start.16 = (s32[2,2]{1,0:T(2,128)}, s32[2,2]{1,0:T(2,128)S(1)}, u32[]{:S(2)}) copy-start(s32[2,2]{1,0:T(2,128)S(1)} %get-tuple-element.176) | copy-start | bytes 52
  235.8 10.4 %collective-permute-start.4 = (f32[512,256]{1,0:T(8,128)S(1)}, f32[512,256]{1,0:T(8,128)S(1)}, u32[]{:S(2)}, u32[]{:S(2)}) collective-permute-start(f32[512,256]{1,0:T(8,128)S(1)} %bitcast_select_fusion.5), channel_id=1, source_target_pairs={{0,2},{1,3},{2,4},{3,5},{4,6},{5,7},{8,10},{9,11},{10,12},{11,13},... | collective-permute-start | bytes 1572872 | tf_op jit(solution)/shard_map/ppermute | solution.py:23
  246.2 7.7 %copy-start.12 = (f32[512,256]{1,0:T(8,128)}, f32[512,256]{1,0:T(8,128)S(1)}, u32[]{:S(2)}) copy-start(f32[512,256]{1,0:T(8,128)S(1)} %collective-permute-done.4) | copy-start | bytes 1572868
  248.3 31.5 %collective-permute-start.5 = (f32[512,256]{1,0:T(8,128)}, f32[512,256]{1,0:T(8,128)}, u32[]{:S(2)}, u32[]{:S(2)}) collective-permute-start(f32[512,256]{1,0:T(8,128)} %bitcast_select_fusion.4), channel_id=1, source_target_pairs={{0,2},{1,3},{2,4},{3,5},{4,6},{5,7},{8,10},{9,11},{10,12},{11,13},... | collective-permute-start | bytes 1572872 | tf_op jit(solution)/shard_map/ppermute | solution.py:23
  256.8 0.7 copy-start.15
  281.7 9.2 %collective-permute-start.6 = (f32[512,256]{1,0:T(8,128)}, f32[512,256]{1,0:T(8,128)}, u32[]{:S(2)}, u32[]{:S(2)}) collective-permute-start(f32[512,256]{1,0:T(8,128)} %bitcast_select_fusion.3), channel_id=1, source_target_pairs={{0,2},{1,3},{2,4},{3,5},{4,6},{5,7},{8,10},{9,11},{10,12},{11,13},... | collective-permute-start | bytes 1572872 | tf_op jit(solution)/shard_map/ppermute | solution.py:23
  286.2 24.1 %copy-start.13 = (f32[512,256]{1,0:T(8,128)S(1)}, f32[512,256]{1,0:T(8,128)}, u32[]{:S(2)}) copy-start(f32[512,256]{1,0:T(8,128)} %copy-done.12) | copy-start | bytes 1572868
  287.1 3.8 copy-start.14
  291.0 13.8 %collective-permute-start.7 = (f32[512,256]{1,0:T(8,128)S(1)}, f32[512,256]{1,0:T(8,128)S(1)}, u32[]{:S(2)}, u32[]{:S(2)}) collective-permute-start(f32[512,256]{1,0:T(8,128)S(1)} %bitcast_select_fusion.2), channel_id=1, source_target_pairs={{0,2},{1,3},{2,4},{3,5},{4,6},{5,7},{8,10},{9,11},{10,12},{11,13},... | collective-permute-start | bytes 1572872 | tf_op jit(solution)/shard_map/ppermute | solution.py:23
  304.8 13.8 %collective-permute-start.8 = (f32[512,256]{1,0:T(8,128)S(1)}, f32[512,256]{1,0:T(8,128)S(1)}, u32[]{:S(2)}, u32[]{:S(2)}) collective-permute-start(f32[512,256]{1,0:T(8,128)S(1)} %bitcast_select_fusion.1), channel_id=1, source_target_pairs={{0,2},{1,3},{2,4},{3,5},{4,6},{5,7},{8,10},{9,11},{10,12},{11,13},... | collective-permute-start | bytes 1572872 | tf_op jit(solution)/shard_map/ppermute | solution.py:23
  310.3 19.5 %copy-start.1 = (f32[16,256,1,256]{3,1,2,0:T(8,128)S(1)}, f32[16,256,1,256]{3,1,2,0:T(8,128)}, u32[]{:S(2)}) copy-start(f32[16,256,1,256]{3,1,2,0:T(8,128)} %copy.13) | copy-start | bytes 12582916
  318.8 11.1 %collective-permute-start.9 = (f32[512,256]{1,0:T(8,128)S(1)}, f32[512,256]{1,0:T(8,128)S(1)}, u32[]{:S(2)}, u32[]{:S(2)}) collective-permute-start(f32[512,256]{1,0:T(8,128)S(1)} %bitcast_select_fusion), channel_id=1, source_target_pairs={{0,2},{1,3},{2,4},{3,5},{4,6},{5,7},{8,10},{9,11},{10,12},{11,13},... | collective-permute-start | bytes 1572872 | tf_op jit(solution)/shard_map/ppermute | solution.py:23
  329.9 2.7 copy-start.3
  332.6 19.4 %copy-start.17 = (s32[2,2]{1,0:T(2,128)S(1)}, s32[2,2]{1,0:T(2,128)}, u32[]{:S(2)}) copy-start(s32[2,2]{1,0:T(2,128)} %copy-done.16) | copy-start | bytes 52
  332.6 58.6 %collective-permute-start.10 = (f32[4096,256]{1,0:T(8,128)}, f32[4096,256]{1,0:T(8,128)}, u32[]{:S(2)}, u32[]{:S(2)}) collective-permute-start(f32[4096,256]{1,0:T(8,128)} %bitcast.27), channel_id=1, source_target_pairs={{0,1},{1,0},{2,3},{3,2},{4,5},{5,4},{6,7},{7,6},{8,9},{9,8},{10,11... | collective-permute-start | bytes 12582920 | tf_op jit(solution)/shard_map/ppermute | solution.py:27
  332.9 48.2 %collective-permute-start.12 = (f32[256,2048]{1,0:T(8,128)S(1)}, f32[256,2048]{1,0:T(8,128)}, u32[]{:S(2)}, u32[]{:S(2)}) collective-permute-start(f32[256,2048]{1,0:T(8,128)S(1)} %broadcast_select_fusion), channel_id=1, source_target_pairs={{0,8},{8,0},{16,24},{24,16},{1,9},{9,1},{17,25},{25,17},{2,10},{10... | collective-permute-start | bytes 6291464 | tf_op jit(solution)/shard_map/ppermute | solution.py:39
  414.5 9.1 %copy-start.10 = (f32[256,512]{1,0:T(8,128)S(1)}, f32[256,512]{1,0:T(8,128)}, u32[]{:S(2)}) copy-start(f32[256,512]{1,0:T(8,128)} %concatenate.14) | copy-start | bytes 1572868
  414.5 9.1 %copy-start.11 = (f32[256,512]{1,0:T(8,128)S(1)}, f32[256,512]{1,0:T(8,128)}, u32[]{:S(2)}) copy-start(f32[256,512]{1,0:T(8,128)} %pad_maximum_fusion.3) | copy-start | bytes 1572868
  423.6 8.5 %copy-start = (f32[512,2048]{1,0:T(8,128)S(1)}, f32[512,2048]{1,0:T(8,128)}, u32[]{:S(2)}) copy-start(f32[512,2048]{1,0:T(8,128)} %pad_maximum_fusion.1.cols_ref) | copy-start | bytes 12582916
Sparse Core Ops, SparseCore 0:
  12.5 133.1 all-reduce.3
